TPU v7x, 512 devices: a whole 4x8x8 slice. The times are simulated.
512 devices in a mesh: img: 32 (over z_hi, y, core), blk: 16 (over z_lo, x).
Axes of the slice: x: 4, y: 8, z: 8 (z_hi: 2, z_lo: 4; z = z_hi * 4 + z_lo), core: 2. Of those that a mesh axis runs over, the one named last changes fastest.
Arguments:
- images: bfloat16 [10240, 2, 20480], P('img', None, 'blk'), may hold values from -70 to 70
- projections: bfloat16 [192, 2, 20480], P(None, None, 'blk'), may hold values from -6 to 6
- ctf_table: float32 [16, 20480], P(None, 'blk'), may hold values from -1 to 1
- ctf_group: int32 [10240], P('img'), may hold values from 0 to 15
- noise_weight: float32 [20480], P('blk'), may hold values from 0.002 to 0.02
- significant: int32 [10240, 48], P('img'), may hold values from 0 to 191, all different within a row
Outputs:
- slices: float32 [192, 2, 20480], P('img', None, 'blk')
- spectrum: float32 [20480], P('blk')
Inputs may be any that keep to these rules, and one draw needn't show every extreme that they name: `significant`: the 48 entries of each row are different orientations.
All inputs are finite; a program needn't handle non-finite values.
Results may differ from a plain program's by a relative error of at most 0.0019.
The roundings to bfloat16 on the way count: a program that leaves them out, or rounds other values in their place, can miss the bound.
Values may be sent and summed in bfloat16 or wider, within the bound.
No kernel may reach another device: no remote copies, remote signals or barrier semaphores. Data moves between devices by JAX's collectives and lax.ppermute only.
A program may use at most 64 MiB of HBM per device.

v0:
```python
import jax
import jax.numpy as jnp
from jax import lax
from jax.sharding import PartitionSpec as P


def weights_of(scores, sig_rows):
    rows = jnp.arange(scores.shape[0], dtype=jnp.int32)[:, None]
    mask = jnp.zeros(scores.shape, jnp.float32).at[rows, sig_rows].set(1.0)
    top = jnp.max(jnp.where(mask > 0, scores, -jnp.inf), axis=1, keepdims=True)
    expo = jnp.exp(jnp.where(mask > 0, scores - top, -jnp.inf))
    return (expo / jnp.sum(expo, axis=1, keepdims=True)).astype(jnp.bfloat16)


def per_device(images, projections, ctf_table, ctf_group, noise_weight, significant):
    img_rows = images.shape[0]
    orient = projections.shape[0]
    k_dev = images.shape[2]
    onehot = (
        ctf_group[:, None] == jnp.arange(ctf_table.shape[0], dtype=jnp.int32)[None, :]
    ).astype(jnp.float32)
    ctf = jnp.dot(onehot, ctf_table, precision=lax.Precision.HIGHEST)
    xf = images.astype(jnp.float32)
    scaled = ctf * noise_weight[None, :]
    left = jnp.concatenate([2.0 * scaled[:, None, :] * xf, (-scaled * ctf)[:, None, :]], axis=1)
    left = left.astype(jnp.bfloat16).reshape(img_rows, 3 * k_dev)
    pf = projections.astype(jnp.float32)
    power = (pf[:, 0] * pf[:, 0] + pf[:, 1] * pf[:, 1]).astype(jnp.bfloat16)
    right = jnp.concatenate([projections, power[:, None, :]], axis=1).reshape(orient, 3 * k_dev)
    partial_value = lax.dot_general(
        left, right, (((1,), (1,)), ((), ())), preferred_element_type=jnp.float32
    )
    scores = lax.psum(partial_value, "blk")
    weights = weights_of(scores, significant)
    mixed = jnp.dot(weights, right, preferred_element_type=jnp.float32).reshape(img_rows, 3, k_dev)
    wsum = jnp.sum(weights.astype(jnp.float32), axis=1)
    noise = wsum[:, None] * (xf[:, 0] * xf[:, 0] + xf[:, 1] * xf[:, 1])
    noise = (
        noise
        - 2.0 * ctf * (xf[:, 0] * mixed[:, 0] + xf[:, 1] * mixed[:, 1])
        + ctf * ctf * mixed[:, 2]
    )
    total_images = img_rows * lax.axis_size("img")
    spectrum = lax.psum(jnp.sum(noise, axis=0), "img") / total_images
    corrected = (ctf[:, None, :] * xf).astype(jnp.bfloat16).reshape(img_rows, 2 * k_dev)
    owned = orient // lax.axis_size("img")
    full = lax.dot_general(
        weights, corrected, (((0,), (0,)), ((), ())), preferred_element_type=jnp.float32
    )
    slices = lax.psum_scatter(full, "img", scatter_dimension=0, tiled=True)
    return (slices.reshape(owned, 2, k_dev), spectrum)


def solution(mesh):
    return jax.shard_map(
        per_device,
        mesh=mesh,
        in_specs=(
            P("img", None, "blk"),
            P(None, None, "blk"),
            P(None, "blk"),
            P("img"),
            P("blk"),
            P("img", None),
        ),
        out_specs=(P("img", None, "blk"), P("blk")),
        check_vma=False,
    )
```

profile of v0, /device:TPU:56, one launch (start us, length us, event | category | flops | bytes accessed | tf_op | source)
XLA Modules:
  0.0 418.5 jit_solution(4772395652314176711)
XLA Ops:
  7.2 1.4 fusion.31
  10.5 1.2 copy-done.2
  11.6 1.8 fusion.5
  13.5 1.8 fusion.16
  18.0 57.5 %scatter_custom_fusion = f32[61440]{0:T(1024)} fusion(s32[15360]{0:T(1024)} %reshape.41, f32[15360]{0:T(1024)S(1)} %broadcast.30, f32[]{:T(128)} %constant.7.clone.1), kind=kCustom, calls=%fused_computation.46 | custom fusion | bytes 246272
  76.5 1.9 copy_convert_fusion
  78.5 1.6 copy.25
  80.1 1.3 dynamic-slice.4
  82.0 96.6 %all-reduce.4.cloned.1.call-done = f32[320,192]{0,1:T(8,128)} async-done(((f32[320,192]{0,1:T(8,128)}), f32[320,192]{0,1:T(8,128)}) %all-reduce.4.cloned.1.call-update) | async-done | bytes 245776 | tf_op jit(solution)/shard_map/psum | solution.py:33
  179.7 1.1 fusion.23
  180.7 1.1 convert_reduce_fusion
  181.8 2.0 fusion.32
  183.8 92.2 %fusion = f32[8,2560]{1,0:T(8,128)S(1)} fusion(f32[192,2560]{1,0:T(8,128)} %fusion.32), kind=kCustom, calls=%all-reduce-scatter | all-reduce-scatter fusion | flops 655361 | bytes 2050048
  276.6 2.2 collective-permute-start.6
  278.8 1.9 collective-permute-start.5
  280.8 3.3 collective-permute-start.4
  284.1 17.1 %collective-permute-start.3 = (f32[8,2560]{1,0:T(8,128)S(1)}, f32[8,2560]{1,0:T(8,128)}, u32[]{:S(2)}, u32[]{:S(2)}) collective-permute-start(f32[8,2560]{1,0:T(8,128)S(1)} %fusion), channel_id=1, source_target_pairs={{0,64},{16,80},{32,96},{48,112},{64,128},{80,144},{96,160},{112,17... | collective-permute-start | bytes 245768
  302.0 1.9 collective-permute-start.7
  304.7 78.4 %psum.15 = f32[1280]{0:T(1024)S(1)} all-reduce(f32[1280]{0:T(1024)S(1)} %fusion.8), channel_id=1, replica_groups=mesh['img'=32,'blk'=16] {'img'}, use_global_device_ids=true, to_apply=%region_7.8 | all-reduce | flops 1280 | bytes 10240 | tf_op jit(solution)/shard_map/psum | solution.py:44
  383.2 8.9 %collective-permute-start.2 = (f32[8,2560]{1,0:T(8,128)S(1)}, f32[8,2560]{1,0:T(8,128)S(1)}, u32[]{:S(2)}, u32[]{:S(2)}) collective-permute-start(f32[8,2560]{1,0:T(8,128)S(1)} %fusion), channel_id=1, source_target_pairs={{0,48},{16,64},{32,80},{48,96},{64,112},{80,128},{96,144},{112,160... | collective-permute-start | bytes 245768
  392.1 9.3 %collective-permute-start.1 = (f32[8,2560]{1,0:T(8,128)S(1)}, f32[8,2560]{1,0:T(8,128)S(1)}, u32[]{:S(2)}, u32[]{:S(2)}) collective-permute-start(f32[8,2560]{1,0:T(8,128)S(1)} %fusion), channel_id=1, source_target_pairs={{0,32},{16,48},{32,64},{48,80},{64,96},{80,112},{96,128},{112,144}... | collective-permute-start | bytes 245768
  401.4 1.9 collective-permute-start
  403.9 3.2 collective-permute-done
  407.1 3.8 concatenate.13
  (54 shorter events, 10.2 us)
Async XLA Ops:
  7.2 1.6 copy-start
  7.2 171.5 %all-reduce.4.cloned.1.call-start = ((), (), s32[]{:S(2)}) async-start(), calls=%async_computation | async-start | bytes 589824 | tf_op jit(solution)/shard_map/psum | solution.py:33
  8.6 4.8 %copy-start.3 = (bf16[192,2,1280]{2,0,1:T(8,128)(2,1)}, bf16[192,2,1280]{2,0,1:T(8,128)(2,1)S(1)}, u32[]{:S(2)}) copy-start(bf16[192,2,1280]{2,0,1:T(8,128)(2,1)S(1)} %get-tuple-element.8) | copy-start | bytes 2949124
  8.6 0.7 copy-start.10
  8.6 1.6 copy-start.9
  9.3 4.1 copy-start.5
  10.2 1.4 copy-start.2
  13.5 1.9 copy-start.8
  13.5 1.9 copy-start.11
  13.5 2.0 copy-start.12
  78.5 101.2 %copy-start.7 = (pred[192,320]{1,0:T(8,128)(4,1)}, pred[192,320]{1,0:T(8,128)(4,1)S(1)}, u32[]{:S(2)}) copy-start(pred[192,320]{1,0:T(8,128)(4,1)S(1)} %reshape.40) | copy-start | bytes 184324
  183.8 117.4 %copy-start.4 = (bf16[192,2,1280]{2,0,1:T(8,128)(2,1)S(1)}, bf16[192,2,1280]{2,0,1:T(8,128)(2,1)}, u32[]{:S(2)}) copy-start(bf16[192,2,1280]{2,0,1:T(8,128)(2,1)} %copy-done.3) | copy-start | bytes 2949124
  183.8 117.4 %copy-start.6 = (bf16[192,1,1280]{2,0,1:T(8,128)(2,1)S(1)}, bf16[192,1,1280]{2,0,1:T(8,128)(2,1)}, u32[]{:S(2)}) copy-start(bf16[192,1,1280]{2,0,1:T(8,128)(2,1)} %copy-done.5) | copy-start | bytes 1474564
  276.6 27.3 %copy-start.1 = (f32[320,2,1280]{2,0,1:T(8,128)S(1)}, f32[320,2,1280]{2,0,1:T(8,128)}, u32[]{:S(2)}) copy-start(f32[320,2,1280]{2,0,1:T(8,128)} %copy_convert_fusion) | copy-start | bytes 9830404
  276.6 115.4 %collective-permute-start.6 = (f32[8,2560]{1,0:T(8,128)S(1)}, f32[8,2560]{1,0:T(8,128)S(1)}, u32[]{:S(2)}, u32[]{:S(2)}) collective-permute-start(f32[8,2560]{1,0:T(8,128)S(1)} %fusion), channel_id=1, source_target_pairs={{0,112},{16,128},{32,144},{48,160},{64,176},{80,192},{96,208},{112... | collective-permute-start | bytes 245768
  278.8 122.5 %collective-permute-start.5 = (f32[8,2560]{1,0:T(8,128)S(1)}, f32[8,2560]{1,0:T(8,128)}, u32[]{:S(2)}, u32[]{:S(2)}) collective-permute-start(f32[8,2560]{1,0:T(8,128)S(1)} %fusion), channel_id=1, source_target_pairs={{0,96},{16,112},{32,128},{48,144},{64,160},{80,176},{96,192},{112,... | collective-permute-start | bytes 245768
  280.8 123.2 %collective-permute-start.4 = (f32[8,2560]{1,0:T(8,128)S(1)}, f32[8,2560]{1,0:T(8,128)}, u32[]{:S(2)}, u32[]{:S(2)}) collective-permute-start(f32[8,2560]{1,0:T(8,128)S(1)} %fusion), channel_id=1, source_target_pairs={{0,80},{16,96},{32,112},{48,128},{64,144},{80,160},{96,176},{112,1... | collective-permute-start | bytes 245768
  284.1 119.8 %collective-permute-start.3 = (f32[8,2560]{1,0:T(8,128)S(1)}, f32[8,2560]{1,0:T(8,128)}, u32[]{:S(2)}, u32[]{:S(2)}) collective-permute-start(f32[8,2560]{1,0:T(8,128)S(1)} %fusion), channel_id=1, source_target_pairs={{0,64},{16,80},{32,96},{48,112},{64,128},{80,144},{96,160},{112,17... | collective-permute-start | bytes 245768
  302.0 81.1 %collective-permute-start.7 = (f32[6,2560]{1,0:T(8,128)}, f32[6,2560]{1,0:T(8,128)S(1)}, u32[]{:S(2)}, u32[]{:S(2)}) collective-permute-start(f32[6,2560]{1,0:T(8,128)} %slice.41), channel_id=1, source_target_pairs={{0,128},{16,144},{32,160},{48,176},{64,192},{80,208},{96,224},{112... | collective-permute-start | bytes 184328
  383.2 20.7 %collective-permute-start.2 = (f32[8,2560]{1,0:T(8,128)S(1)}, f32[8,2560]{1,0:T(8,128)S(1)}, u32[]{:S(2)}, u32[]{:S(2)}) collective-permute-start(f32[8,2560]{1,0:T(8,128)S(1)} %fusion), channel_id=1, source_target_pairs={{0,48},{16,64},{32,80},{48,96},{64,112},{80,128},{96,144},{112,160... | collective-permute-start | bytes 245768
  392.1 11.8 %collective-permute-start.1 = (f32[8,2560]{1,0:T(8,128)S(1)}, f32[8,2560]{1,0:T(8,128)S(1)}, u32[]{:S(2)}, u32[]{:S(2)}) collective-permute-start(f32[8,2560]{1,0:T(8,128)S(1)} %fusion), channel_id=1, source_target_pairs={{0,32},{16,48},{32,64},{48,80},{64,96},{80,112},{96,128},{112,144}... | collective-permute-start | bytes 245768
  401.4 5.8 %collective-permute-start = (f32[8,2560]{1,0:T(8,128)S(1)}, f32[8,2560]{1,0:T(8,128)S(1)}, u32[]{:S(2)}, u32[]{:S(2)}) collective-permute-start(f32[8,2560]{1,0:T(8,128)S(1)} %fusion), channel_id=1, source_target_pairs={{0,16},{16,32},{32,48},{48,64},{64,80},{80,96},{96,112},{112,128},... | collective-permute-start | bytes 245768
Sparse Core Ops, SparseCore 0:
  15.5 163.1 all-reduce.3
where the time goes:
time: 419 us; the launch traced here: 418 us
  blocking collectives  171 us (41%)
  waiting for transfers between devices  99.9 us (24%)
  local copies, waits for them, and re-layouts  69.1 us (16%)
  starting transfers between devices  46.5 us (11%)
  between operations  15 us (4%)
  other arithmetic  11.8 us (3%)
  matrix products  5.51 us (1%)
    psum x1, waiting for transfers between devices, per_device(): scores = lax.psum(partial_value, 'blk')  96.6 us
    unnamed x1, blocking collectives  92.2 us
    psum x1, blocking collectives, per_device(): spectrum = lax.psum(jnp.sum(noise, axis=0), 'img') / total_images  78.4 us
    unnamed x34, local copies, waits for them, and re-layouts  66.7 us
    unnamed x8, starting transfers between devices  46.5 us
  transfers between devices with their start and end apart: 9, of which 2 were waited for; matrix products, arithmetic and copies ran while one was open for 16% of the time, Pallas kernels for 0%

commit v1 on v0

v1 whole, which is shorter than its diff:
```python
import jax
import jax.numpy as jnp
from jax import lax
from jax.experimental import pallas as pl
from jax.experimental.pallas import tpu as pltpu
from jax.sharding import PartitionSpec as P

NX, NZ, NY = 4, 4, 8
TOP = 13.0
F32 = jnp.float32
BF16 = jnp.bfloat16
F16 = jnp.float16
PARAMS = pltpu.CompilerParams(vmem_limit_bytes=40 * 1024 * 1024)


def thirds(v):
    hi = v.astype(BF16)
    rest = v - hi.astype(F32)
    mid = rest.astype(BF16)
    low = (rest - mid.astype(F32)).astype(BF16)
    return jnp.concatenate([hi, mid, low], axis=0)


def matmul(a, b, dims):
    return lax.dot_general(a, b, (dims, ((), ())), preferred_element_type=F32)


def exponent(v):
    top = jnp.maximum(jnp.max(jnp.max(jnp.abs(v), axis=0, keepdims=True), axis=1, keepdims=True), 1e-30)
    return jnp.floor(jnp.log(top) * 1.4426950408889634)


def pre_kernel(xi, pi, table, grp, noise, sig_t, compact, corr_out, q2_out, prj_out, left, ctf, corr, q2, prj, sems):
    groups, k_dev = table.shape
    n_img = ctf.shape[0]
    orient = prj.shape[0]
    n_sig = sig_t.shape[0]
    onehot = (grp[...] == lax.broadcasted_iota(jnp.int32, (groups, n_img), 0)).astype(F32).astype(BF16)
    ctf[...] = matmul(jnp.concatenate([onehot] * 3, axis=0), thirds(table[...]), ((0,), (0,)))
    for row in range(0, n_img, 32):
        rows = slice(row, row + 32)
        x0 = xi[0, rows].astype(F32)
        x1 = xi[1, rows].astype(F32)
        c = ctf[rows]
        scaled = c * noise[...]
        twice = 2.0 * scaled
        left[rows, :k_dev] = (twice * x0).astype(BF16)
        left[rows, k_dev : 2 * k_dev] = (twice * x1).astype(BF16)
        left[rows, 2 * k_dev :] = (-scaled * c).astype(BF16)
        corr[rows, :k_dev] = (c * x0).astype(BF16)
        corr[rows, k_dev:] = (c * x1).astype(BF16)
        q2[rows] = x0 * x0 + x1 * x1
    for row in range(0, orient, 32):
        rows = slice(row, row + 32)
        prj[rows, :k_dev] = pi[0, rows]
        prj[rows, k_dev : 2 * k_dev] = pi[1, rows]
        p0 = pi[0, rows].astype(F32)
        p1 = pi[1, rows].astype(F32)
        prj[rows, 2 * k_dev :] = (p0 * p0 + p1 * p1).astype(BF16)
    copies = [
        pltpu.make_async_copy(src, dst, sems.at[n])
        for n, (src, dst) in enumerate(((corr, corr_out), (q2, q2_out), (prj, prj_out)))
    ]
    for copy in copies:
        copy.start()
    part = matmul(left[...], prj[...], ((1,), (1,)))
    sig_pad = jnp.concatenate([sig_t[...], jnp.zeros((128 - n_sig, n_img), jnp.int32)], axis=0)
    index = sig_pad.T
    first = jnp.take_along_axis(part[:, :128], jnp.minimum(index, 127), axis=1)
    rest = jnp.concatenate([part[:, 128:], jnp.zeros((n_img, 256 - orient), F32)], axis=1)
    second = jnp.take_along_axis(rest, jnp.maximum(index - 128, 0), axis=1)
    picked = jnp.where(index < 128, first, second).T[:n_sig]
    short = n_sig // 2
    for n in range(NX):
        compact[n, :n_sig] = picked[:, :128]
        compact[n, n_sig : 2 * n_sig] = picked[:, 128:256]
        compact[n, 2 * n_sig :, :64] = picked[:short, 256:]
        compact[n, 2 * n_sig :, 64:] = picked[short:, 256:]
    for copy in copies:
        copy.wait()


def relay_kernel(stack, out):
    total = (stack[0] + stack[2]) + (stack[1] + stack[3])
    for n in range(NZ):
        out[n] = total


def mid_kernel(stack, sig_t, corr_in, q2_in, prj_in, table, grp, target, total, away, mine, corr, q2, prj, sems):
    copies = [
        pltpu.make_async_copy(src, dst, sems.at[n])
        for n, (src, dst) in enumerate(((corr_in, corr), (q2_in, q2), (prj_in, prj)))
    ]
    for copy in copies:
        copy.start()
    groups, k_dev = table.shape
    n_sig, n_img = sig_t.shape
    orient = prj.shape[0]
    half = orient // 2
    packed = (stack[0] + stack[2]) + (stack[1] + stack[3])
    last = packed[2 * n_sig :]
    scores = jnp.concatenate(
        [packed[:n_sig], packed[n_sig : 2 * n_sig], jnp.concatenate([last[:, :64], last[:, 64:]], axis=0)], axis=1
    )
    expo = jnp.exp(scores - jnp.max(scores, axis=0, keepdims=True))
    w_c = (expo / jnp.sum(expo, axis=0, keepdims=True)).astype(BF16).astype(F32)
    sig = sig_t[...]
    blocks = []
    for base in range(0, orient, 64):
        ids = lax.broadcasted_iota(jnp.int32, (64, n_img), 0) + base
        acc = jnp.zeros((64, n_img), F32)
        for s in range(n_sig):
            acc = jnp.where(sig[s : s + 1] == ids, w_c[s : s + 1], acc)
        blocks.append(acc.astype(BF16))
    w_t = jnp.concatenate(blocks, axis=0)
    shuffle = (target[...] == lax.broadcasted_iota(jnp.int32, (orient, orient), 1)).astype(F32).astype(BF16)
    w_s = matmul(shuffle, w_t, ((1,), (0,))).astype(BF16)
    w_sum = matmul(w_t, jnp.ones((orient, 128), BF16), ((0,), (0,)))
    onehot = (grp[...] == lax.broadcasted_iota(jnp.int32, (groups, n_img), 0)).astype(F32).astype(BF16)
    w_g = matmul(onehot, w_t, ((1,), (1,)))
    for copy in copies:
        copy.wait()
    away[:half] = matmul(w_s[:half], corr[...], ((1,), (0,)))
    mine[:half] = matmul(w_s[half:], corr[...], ((1,), (0,)))
    mix = matmul(thirds(w_g), prj[:, 2 * k_dev :], ((1,), (0,)))
    mix = (mix[:groups] + mix[groups : 2 * groups]) + mix[2 * groups :]
    noise = jnp.sum(table[...] * table[...] * mix, axis=0, keepdims=True)
    plain = [
        jnp.sum(q2[:, at : at + 128] * w_sum, axis=0, keepdims=True) for at in range(0, k_dev, 128)
    ]
    noise = noise + jnp.concatenate(plain, axis=1)
    for c in range(2):
        at = c * k_dev
        right = matmul(shuffle, prj[:, at : at + k_dev], ((1,), (0,)))
        cross = jnp.sum(right[:half] * away[:half, at : at + k_dev], axis=0, keepdims=True)
        cross = cross + jnp.sum(right[half:] * mine[:half, at : at + k_dev], axis=0, keepdims=True)
        noise = noise - 2.0 * cross
    noise = noise * (1.0 / total)
    for ref in (away, mine):
        ref[half:] = jnp.zeros((8, 2 * k_dev), F32)
        ref[half : half + 1, :k_dev] = noise


def pack_kernel(mine, got, chunks):
    half = mine.shape[0] - 8
    k_dev = mine.shape[1] // 2
    main = 3 * k_dev // 2
    bit = k_dev // 2
    own = half // (2 * NY)
    data = mine[:half] + got[:half]
    tail = mine[half : half + 1, :k_dev] + got[half : half + 1, :k_dev]
    e_half = exponent(data)
    e_tail = exponent(tail)
    data = data * jnp.exp2(TOP - e_half)
    tail = tail * jnp.exp2(TOP - e_tail)
    wide = k_dev // 5
    side = [tail[:, n * wide : (n + 1) * wide] for n in range(5)]
    side = side + [jnp.broadcast_to(v, (1, wide)) for v in (e_half, e_tail, e_tail)]
    side = jnp.concatenate(side, axis=0)
    for d in range(2 * NY):
        rows = data[own * d : own * d + own]
        chunks[d, :own, :main] = rows[:, :main]
        for n in range(own):
            chunks[d, own + n // 3 : own + n // 3 + 1, n % 3 * bit : n % 3 * bit + bit] = rows[n : n + 1, main:]
        chunks[d, :, main:] = side


def end_kernel(owned, chunks, slices, spectrum):
    k_dev = slices.shape[2]
    main = 3 * k_dev // 2
    bit = k_dev // 2
    data = jnp.zeros((8, main), F32)
    tail = jnp.zeros((8, k_dev // 5), F32)
    for d in range(2 * NY):
        side = chunks[d, :, main:]
        data = data + chunks[d, :, :main] * jnp.exp2(side[5:6, :1] - TOP)
        tail = tail + side * jnp.exp2(side[6:7, :1] - TOP)
    slices[:, 0, :] = data[:owned, :k_dev]
    slices[:, 1, :bit] = data[:owned, k_dev:]
    for n in range(owned):
        slices[n : n + 1, 1, bit:] = data[owned + n // 3 : owned + n // 3 + 1, n % 3 * bit : n % 3 * bit + bit]
    spectrum[...] = jnp.concatenate([tail[n : n + 1] for n in range(5)], axis=1)


VM = pl.BlockSpec(memory_space=pltpu.VMEM)
HB = pl.BlockSpec(memory_space=pltpu.HBM)


def call(body, ins, outs, scratch=()):
    shapes = [jax.ShapeDtypeStruct(s, t) for s, t, _ in outs]
    return pl.pallas_call(
        body,
        in_specs=ins,
        out_specs=[where for _, _, where in outs],
        out_shape=shapes,
        scratch_shapes=list(scratch),
        compiler_params=PARAMS,
    )


def spread(v, axis, groups=None):
    return lax.all_to_all(v, axis, 0, 0, axis_index_groups=groups, tiled=True)


def img_shift(v, dh, dc):
    perm = []
    for h in range(2):
        for y in range(NY):
            for c in range(2):
                perm.append(((h * NY + y) * 2 + c, ((h + dh) % 2 * NY + y) * 2 + (c + dc) % 2))
    return lax.ppermute(v, "img", perm)


def pre(images, projections, ctf_table, grp, noise_weight, sig_t):
    n_img, _, k_dev = images.shape
    orient = projections.shape[0]
    carried = [((n_img, 2 * k_dev), BF16), ((n_img, k_dev), F32), ((orient, 3 * k_dev), BF16)]
    packed = (NX, sig_t.shape[0] * n_img // 128, 128)
    return call(
        pre_kernel,
        [VM] * 6,
        [(packed, F32, VM)] + [(s, t, HB) for s, t in carried],
        [pltpu.VMEM((n_img, 3 * k_dev), BF16), pltpu.VMEM((n_img, k_dev), F32)]
        + [pltpu.VMEM(s, t) for s, t in carried]
        + [pltpu.SemaphoreType.DMA((3,))],
    )(
        images.transpose(1, 0, 2),
        projections.transpose(1, 0, 2),
        ctf_table,
        grp,
        noise_weight[None],
        sig_t,
    )


def mid(stack, sig_t, corr, q2, prj, ctf_table, grp, target, total):
    orient, k_dev = prj.shape[0], ctf_table.shape[1]

    def body(*refs):
        mid_kernel(*refs[:8], total, *refs[8:])

    shape = ((orient // 2 + 8, 2 * k_dev), F32, VM)
    return call(
        body,
        [VM, VM, HB, HB, HB, VM, VM, VM],
        [shape, shape],
        [pltpu.VMEM(v.shape, v.dtype) for v in (corr, q2, prj)] + [pltpu.SemaphoreType.DMA((3,))],
    )(stack, sig_t, corr, q2, prj, ctf_table, grp, target)


def targets(me, orient, owned):
    pos = jnp.arange(orient, dtype=jnp.int32)
    a, h = pos // (orient // 2), pos % (orient // 2)
    owner = h // owned * 2 + (me + 1 - a) % 2
    return (owner * owned + h % owned)[:, None]


def per_device(images, projections, ctf_table, ctf_group, noise_weight, significant):
    img_rows, _, k_dev = images.shape
    orient = projections.shape[0]
    owned = orient // lax.axis_size("img")
    total = img_rows * lax.axis_size("img")
    grp = ctf_group[None]
    sig_t = significant.T
    compact, corr, q2, prj = pre(images, projections, ctf_table, grp, noise_weight, sig_t)
    along_x = [[z * NX + x for x in range(NX)] for z in range(NZ)]
    along_z = [[z * NX + x for z in range(NZ)] for x in range(NX)]
    compact = spread(compact, "blk", along_x)
    compact = call(relay_kernel, [VM], [(compact.shape, F32, VM)])(compact)[0]
    stack = spread(compact, "blk", along_z)
    target = targets(lax.axis_index("img"), orient, owned)
    away, mine = mid(stack, sig_t, corr, q2, prj, ctf_table, grp, target, total)
    got = img_shift(away, 0, 1)
    shape = (2 * NY, 8, 3 * k_dev // 2 + k_dev // 5)
    chunks = call(pack_kernel, [VM, VM], [(shape, F32, VM)])(mine, got)[0].astype(F16)
    peers = [[n * 2 + c for n in range(2 * NY)] for c in range(2)]
    chunks = spread(chunks, "img", peers).astype(F32)

    def body(*refs):
        end_kernel(owned, *refs)

    slices, spectrum = call(body, [VM], [((owned, 2, k_dev), F32, VM), ((1, k_dev), F32, VM)])(chunks)
    return (slices, spectrum[0])


def solution(mesh):
    return jax.shard_map(
        per_device,
        mesh=mesh,
        in_specs=(
            P("img", None, "blk"),
            P(None, None, "blk"),
            P(None, "blk"),
            P("img"),
            P("blk"),
            P("img", None),
        ),
        out_specs=(P("img", None, "blk"), P("blk")),
        check_vma=False,
    )
```

time: 419 us -> 82.8 us (0.20)
  the two profiles are of different devices: /device:TPU:56 before, /device:TPU:2 now
where the time goes in v1:
time: 82.8 us; the launch traced here: 82.3 us
  blocking collectives  49.1 us (59%)
  local copies, waits for them, and re-layouts  9.11 us (11%)
  waiting for transfers between devices  8.59 us (10%)
  Pallas kernels  7.67 us (9%)
  starting transfers between devices  5.53 us (7%)
  other arithmetic  1.59 us (2%)
    all_to_all x2, blocking collectives, spread(): return lax.all_to_all(v, axis, 0, 0, axis_index_groups=groups, tiled=True)  49.1 us
    unnamed x22, local copies, waits for them, and re-layouts  8.42 us
    all_to_all x1, waiting for transfers between devices, spread(): return lax.all_to_all(v, axis, 0, 0, axis_index_groups=groups, tiled=True)  5.94 us
    all_to_all x1, starting transfers between devices, spread(): return lax.all_to_all(v, axis, 0, 0, axis_index_groups=groups, tiled=True)  3.61 us
    pallas_call x1, Pallas kernels, pre(): call(pre_kernel, [VM] * 6, [(packed, F32, VM)] + [(s, t, HB) for s, t in...  3.25 us
    pallas_call x1, Pallas kernels, mid(): call(body, [VM, VM, HB, HB, HB, VM, VM, VM], [shape, shape], [pltpu.VMEM(...  3.23 us
    ppermute x1, waiting for transfers between devices, img_shift(): return lax.ppermute(v, 'img', perm)  2.65 us
    ppermute x1, starting transfers between devices, img_shift(): return lax.ppermute(v, 'img', perm)  1.92 us
  transfers between devices with their start and end apart: 2, of which 2 were waited for; matrix products, arithmetic and copies ran while one was open for 1% of the time, Pallas kernels for 0%

profile of v1, /device:TPU:2, one launch (start us, length us, event | category | flops | bytes accessed | tf_op | source)
XLA Modules:
  0.0 82.3 jit_solution(5328646645220089201)
XLA Ops:
  0.6 0.7 broadcast_in_dim.7.grp.refs_6_
  1.3 1.7 %copy.12 = bf16[320,2,1280]{2,0,1:T(8,128)(2,1)S(1)} copy(bf16[320,2,1280]{2,1,0:T(2,128)(2,1)} %param.6) | data formatting | bytes 3276800 | tf_op args[0]
  3.0 0.1 copy.13
  3.1 0.6 copy-done.9
  3.7 0.2 copy-done.4
  4.0 3.2 %shard_map.77 = (f32[4,120,128]{2,1,0:T(8,128)S(1)}, bf16[320,2560]{1,0:T(8,128)(2,1)S(1)}, f32[320,1280]{1,0:T(8,128)S(1)}, bf16[192,3840]{1,0:T(8,128)(2,1)S(1)}) custom-call(bf16[2,320,1280]{2,1,0:T(8,128)(2,1)S(1)} %bitcast.7, bf16[2,192,1280]{2,1,0:T(8,128)(2,1)S(1)} %bitcast.8, f32[16,1280]{1,0:T(8,128)S(1)} %copy-done.4, ...), custom_call_target="tpu_custom_call" | custom-call | tf_op jit(solution)/shard_map/pallas_call | solution.py:219
  7.2 1.1 %copy-done = bf16[192,3840]{1,0:T(8,128)(2,1)} copy-done((bf16[192,3840]{1,0:T(8,128)(2,1)}, bf16[192,3840]{1,0:T(8,128)(2,1)S(1)}, u32[]{:S(2)}) %copy-start) | copy-done | bytes 1474584
  8.3 13.4 %all_to_all.15.stack = f32[4,120,128]{2,1,0:T(8,128)S(1)} all-to-all(f32[4,120,128]{2,1,0:T(8,128)S(1)} %get-tuple-element.10), channel_id=1, replica_groups={{0,1,2,3},{4,5,6,7},{8,9,10,11},{12,13,14,15},{16,17,18,19},{20,21,22,2..., dimensions={0} | all-to-all | bytes 491520 | tf_op jit(solution)/shard_map/all_to_all | solution.py:202
  21.8 0.7 copy-done.2
  22.4 3.6 %all-to-all-start.1 = ((f32[4,120,128]{2,1,0:T(8,128)}), f32[4,120,128]{2,1,0:T(8,128)S(1)}, u32[]{:S(2)}, u32[]{:S(2)}) async-start(f32[4,120,128]{2,1,0:T(8,128)} %copy-done.2), calls=%async_computation.1 | async-start | bytes 491520 | tf_op jit(solution)/shard_map/all_to_all | solution.py:202
  26.1 0.8 %fusion.4.refs_7_ = s32[192,1]{1,0:T(8,128)} fusion(s32[]{:T(128)S(6)} %add.77), kind=kLoop, calls=%fused_computation.15 | loop fusion | flops 7680 | bytes 772 | tf_op jit(solution)/shard_map/add | solution.py:255
  26.9 5.9 %all-to-all-done.1.refs_0_ = f32[4,120,128]{2,1,0:T(8,128)S(1)} async-done(((f32[4,120,128]{2,1,0:T(8,128)}), f32[4,120,128]{2,1,0:T(8,128)S(1)}, u32[]{:S(2)}, u32[]{:S(2)}) %all-to-all-start.1) | async-done | bytes 245792 | tf_op jit(solution)/shard_map/all_to_all | solution.py:202
  32.8 1.4 %copy-done.1 = bf16[192,3840]{1,0:T(8,128)(2,1)S(1)} copy-done((bf16[192,3840]{1,0:T(8,128)(2,1)S(1)}, bf16[192,3840]{1,0:T(8,128)(2,1)}, u32[]{:S(2)}) %copy-start.1) | copy-done | bytes 1474584
  34.2 0.9 %copy-done.3 = s32[192,1]{1,0:T(8,128)S(1)} copy-done((s32[192,1]{1,0:T(8,128)S(1)}, s32[192,1]{1,0:T(8,128)}, u32[]{:S(2)}) %copy-start.3) | copy-done | bytes 792
  35.1 0.9 %copy-done.5 = f32[16,1280]{1,0:T(8,128)S(1)} copy-done((f32[16,1280]{1,0:T(8,128)S(1)}, f32[16,1280]{1,0:T(8,128)}, u32[]{:S(2)}) %copy-start.5) | copy-done | bytes 81944
  36.0 0.9 %copy-done.7 = s32[320,48]{0,1:T(8,128)S(1)} copy-done((s32[320,48]{0,1:T(8,128)S(1)}, s32[320,48]{0,1:T(8,128)}, u32[]{:S(2)}) %copy-start.7) | copy-done | bytes 61464
  36.9 3.2 %shard_map.79 = (f32[104,2560]{1,0:T(8,128)S(1)}, f32[104,2560]{1,0:T(8,128)S(1)}) custom-call(f32[4,120,128]{2,1,0:T(8,128)S(1)} %all-to-all-done.1.refs_0_, s32[48,320]{1,0:T(8,128)S(1)} %bitcast.10, bf16[320,2560]{1,0:T(8,128)(2,1)S(1)} %get-tuple-element.11.refs_2_, f32[320,1280]{1,0:T(8,128)S(1)} %get-tuple-element.12.refs_3_, ...), custom_call_target="tpu_custom_call" | custom-call | tf_op jit(solution)/shard_map/pallas_call | solution.py:243
  40.1 1.9 %collective-permute-start = (f32[104,2560]{1,0:T(8,128)S(1)}, f32[104,2560]{1,0:T(8,128)S(1)}, u32[]{:S(2)}, u32[]{:S(2)}) collective-permute-start(f32[104,2560]{1,0:T(8,128)S(1)} %get-tuple-element.15), channel_id=1, source_target_pairs={{0,16},{16,0},{32,48},{48,32},{64,80},{80,64},{96,112},{112,96},{1... | collective-permute-start | bytes 3194888 | tf_op jit(solution)/shard_map/ppermute | solution.py:211
  42.0 2.6 %collective-permute-done.got = f32[104,2560]{1,0:T(8,128)S(1)} collective-permute-done((f32[104,2560]{1,0:T(8,128)S(1)}, f32[104,2560]{1,0:T(8,128)S(1)}, u32[]{:S(2)}, u32[]{:S(2)}) %collective-permute-start) | collective-permute-done | bytes 1064992 | tf_op jit(solution)/shard_map/ppermute | solution.py:211
  44.7 0.4 shard_map.80
  45.2 35.7 %all_to_all.16 = f16[16,8,2176]{2,1,0:T(8,128)(2,1)S(1)} all-to-all(f16[16,8,2176]{2,1,0:T(8,128)(2,1)S(1)} %convert_element_type.6), channel_id=1, replica_groups={{0,32,64,96,128,160,192,224,256,288,320,352,384,416,448,480},{16,48,80,..., dimensions={0} | all-to-all | bytes 1114112 | tf_op jit(solution)/shard_map/all_to_all | solution.py:202
  80.8 0.1 convert_element_type.7.refs_0_
  80.9 0.8 shard_map.81
  81.7 0.6 reduce
  (15 shorter events, 0.2 us)
Async XLA Ops:
  1.3 1.7 %copy-start.8 = (bf16[192,2,1280]{2,1,0:T(2,128)(2,1)S(1)}, bf16[192,2,1280]{2,1,0:T(2,128)(2,1)}, u32[]{:S(2)}) copy-start(bf16[192,2,1280]{2,1,0:T(2,128)(2,1)} %param.7) | copy-start | bytes 2949124
  3.0 0.7 copy-start.9
  3.0 0.9 %copy-start.4 = (f32[16,1280]{1,0:T(8,128)S(1)}, f32[16,1280]{1,0:T(8,128)}, u32[]{:S(2)}) copy-start(f32[16,1280]{1,0:T(8,128)} %refs_5_.1) | copy-start | bytes 245764
  3.0 0.9 %copy-start.6 = (s32[320,48]{0,1:T(8,128)S(1)}, s32[320,48]{0,1:T(8,128)}, u32[]{:S(2)}) copy-start(s32[320,48]{0,1:T(8,128)} %param.11) | copy-start | bytes 184324
  7.2 1.1 %copy-start = (bf16[192,3840]{1,0:T(8,128)(2,1)}, bf16[192,3840]{1,0:T(8,128)(2,1)S(1)}, u32[]{:S(2)}) copy-start(bf16[192,3840]{1,0:T(8,128)(2,1)S(1)} %get-tuple-element.13.refs_4_) | copy-start | bytes 4423684
  21.8 0.7 copy-start.2
  22.4 10.4 %all-to-all-start.1 = ((f32[4,120,128]{2,1,0:T(8,128)}), f32[4,120,128]{2,1,0:T(8,128)S(1)}, u32[]{:S(2)}, u32[]{:S(2)}) async-start(f32[4,120,128]{2,1,0:T(8,128)} %copy-done.2), calls=%async_computation.1 | async-start | bytes 491520 | tf_op jit(solution)/shard_map/all_to_all | solution.py:202
  32.8 1.4 %copy-start.1 = (bf16[192,3840]{1,0:T(8,128)(2,1)S(1)}, bf16[192,3840]{1,0:T(8,128)(2,1)}, u32[]{:S(2)}) copy-start(bf16[192,3840]{1,0:T(8,128)(2,1)} %copy-done) | copy-start | bytes 4423684
  34.2 0.9 %copy-start.3 = (s32[192,1]{1,0:T(8,128)S(1)}, s32[192,1]{1,0:T(8,128)}, u32[]{:S(2)}) copy-start(s32[192,1]{1,0:T(8,128)} %fusion.4.refs_7_) | copy-start | bytes 2308
  35.1 0.9 %copy-start.5 = (f32[16,1280]{1,0:T(8,128)S(1)}, f32[16,1280]{1,0:T(8,128)}, u32[]{:S(2)}) copy-start(f32[16,1280]{1,0:T(8,128)} %refs_5_.1) | copy-start | bytes 245764
  36.0 0.9 %copy-start.7 = (s32[320,48]{0,1:T(8,128)S(1)}, s32[320,48]{0,1:T(8,128)}, u32[]{:S(2)}) copy-start(s32[320,48]{0,1:T(8,128)} %param.11) | copy-start | bytes 184324
  40.1 4.6 %collective-permute-start = (f32[104,2560]{1,0:T(8,128)S(1)}, f32[104,2560]{1,0:T(8,128)S(1)}, u32[]{:S(2)}, u32[]{:S(2)}) collective-permute-start(f32[104,2560]{1,0:T(8,128)S(1)} %get-tuple-element.15), channel_id=1, source_target_pairs={{0,16},{16,0},{32,48},{48,32},{64,80},{80,64},{96,112},{112,96},{1... | collective-permute-start | bytes 3194888 | tf_op jit(solution)/shard_map/ppermute | solution.py:211

commit v2 on v1

v2 whole, which is shorter than its diff:
```python
import jax
import jax.numpy as jnp
from jax import lax
from jax.experimental import pallas as pl
from jax.experimental.pallas import tpu as pltpu
from jax.sharding import PartitionSpec as P

NX, NZ, NY = 4, 4, 8
TOP = 13.0
F32 = jnp.float32
BF16 = jnp.bfloat16
F16 = jnp.float16
PARAMS = pltpu.CompilerParams(vmem_limit_bytes=24 * 1024 * 1024)


def thirds(v):
    hi = v.astype(BF16)
    rest = v - hi.astype(F32)
    mid = rest.astype(BF16)
    low = (rest - mid.astype(F32)).astype(BF16)
    return jnp.concatenate([hi, mid, low], axis=0)


def matmul(a, b, dims):
    return lax.dot_general(a, b, (dims, ((), ())), preferred_element_type=F32)


def exponent(v):
    top = jnp.maximum(jnp.max(jnp.max(jnp.abs(v), axis=0, keepdims=True), axis=1, keepdims=True), 1e-30)
    return jnp.floor(jnp.log(top) * 1.4426950408889634)


def pre_kernel(xi, pi, table, grp, noise, sig_t, compact, corr, q2, prj, left, ctf):
    groups, k_dev = table.shape
    n_img = ctf.shape[0]
    orient = prj.shape[0]
    n_sig = sig_t.shape[0]
    onehot = (grp[...][None, :] == lax.broadcasted_iota(jnp.int32, (groups, n_img), 0)).astype(F32).astype(BF16)
    weight = noise[...][None, :]
    ctf[...] = matmul(jnp.concatenate([onehot] * 3, axis=0), thirds(table[...]), ((0,), (0,)))
    for row in range(0, n_img, 32):
        rows = slice(row, row + 32)
        x0 = xi[0, rows].astype(F32)
        x1 = xi[1, rows].astype(F32)
        c = ctf[rows]
        scaled = c * weight
        twice = 2.0 * scaled
        left[rows, :k_dev] = (twice * x0).astype(BF16)
        left[rows, k_dev : 2 * k_dev] = (twice * x1).astype(BF16)
        left[rows, 2 * k_dev :] = (-scaled * c).astype(BF16)
        corr[rows, :k_dev] = (c * x0).astype(BF16)
        corr[rows, k_dev:] = (c * x1).astype(BF16)
        q2[rows] = x0 * x0 + x1 * x1
    for row in range(0, orient, 32):
        rows = slice(row, row + 32)
        prj[rows, :k_dev] = pi[0, rows]
        prj[rows, k_dev : 2 * k_dev] = pi[1, rows]
        p0 = pi[0, rows].astype(F32)
        p1 = pi[1, rows].astype(F32)
        prj[rows, 2 * k_dev :] = (p0 * p0 + p1 * p1).astype(BF16)
    part = matmul(left[...], prj[...], ((1,), (1,)))
    sig_pad = jnp.concatenate([sig_t[...], jnp.zeros((128 - n_sig, n_img), jnp.int32)], axis=0)
    index = sig_pad.T
    first = jnp.take_along_axis(part[:, :128], jnp.minimum(index, 127), axis=1)
    rest = jnp.concatenate([part[:, 128:], jnp.zeros((n_img, 256 - orient), F32)], axis=1)
    second = jnp.take_along_axis(rest, jnp.maximum(index - 128, 0), axis=1)
    picked = jnp.where(index < 128, first, second).T[:n_sig]
    short = n_sig // 2
    for n in range(NX):
        compact[n, :n_sig] = picked[:, :128]
        compact[n, n_sig : 2 * n_sig] = picked[:, 128:256]
        compact[n, 2 * n_sig :, :64] = picked[:short, 256:]
        compact[n, 2 * n_sig :, 64:] = picked[short:, 256:]


def relay_kernel(stack, out):
    total = (stack[0] + stack[2]) + (stack[1] + stack[3])
    for n in range(NZ):
        out[n] = total


def targets(me, orient, owned):
    my_h, my_c = me // (2 * NY), me % 2
    pos = lax.broadcasted_iota(jnp.int32, (orient, orient), 0)
    a = jnp.where(pos < orient // 2, 0, 1)
    h = pos - a * (orient // 2)
    d = jnp.where(h < 8 * NY, h >> 3, (h - 8 * NY) >> 2)
    q = jnp.where(h < 8 * NY, h & 7, 8 + (h & 3))
    b = jnp.where(q < owned, 0, 1)
    owner = (((my_h + 1 - b) & 1) * NY + d) * 2 + ((my_c + 1 - a) & 1)
    return owner * owned + q - b * owned


def mid_kernel(stack, sig_t, corr, q2, prj, table, grp, total, away, mine):
    groups, k_dev = table.shape
    n_sig, n_img = sig_t.shape
    orient = prj.shape[0]
    half = orient // 2
    packed = (stack[0] + stack[2]) + (stack[1] + stack[3])
    last = packed[2 * n_sig :]
    scores = jnp.concatenate(
        [packed[:n_sig], packed[n_sig : 2 * n_sig], jnp.concatenate([last[:, :64], last[:, 64:]], axis=0)], axis=1
    )
    expo = jnp.exp(scores - jnp.max(scores, axis=0, keepdims=True))
    w_c = (expo / jnp.sum(expo, axis=0, keepdims=True)).astype(BF16).astype(F32)
    sig = sig_t[...]
    blocks = []
    for base in range(0, orient, 64):
        ids = lax.broadcasted_iota(jnp.int32, (64, n_img), 0) + base
        acc = jnp.zeros((64, n_img), F32)
        for s in range(n_sig):
            acc = jnp.where(sig[s : s + 1] == ids, w_c[s : s + 1], acc)
        blocks.append(acc.astype(BF16))
    w_t = jnp.concatenate(blocks, axis=0)
    target = targets(lax.axis_index("img"), orient, orient // (4 * NY))
    shuffle = (target == lax.broadcasted_iota(jnp.int32, (orient, orient), 1)).astype(F32).astype(BF16)
    w_s = matmul(shuffle, w_t, ((1,), (0,))).astype(BF16)
    w_sum = matmul(w_t, jnp.ones((orient, 128), BF16), ((0,), (0,)))
    onehot = (grp[...][None, :] == lax.broadcasted_iota(jnp.int32, (groups, n_img), 0)).astype(F32).astype(BF16)
    w_g = matmul(onehot, w_t, ((1,), (1,)))
    away[:half] = matmul(w_s[:half], corr[...], ((1,), (0,)))
    mine[:half] = matmul(w_s[half:], corr[...], ((1,), (0,)))
    mix = matmul(thirds(w_g), prj[:, 2 * k_dev :], ((1,), (0,)))
    mix = (mix[:groups] + mix[groups : 2 * groups]) + mix[2 * groups :]
    noise = jnp.sum(table[...] * table[...] * mix, axis=0, keepdims=True)
    plain = [
        jnp.sum(q2[:, at : at + 128] * w_sum, axis=0, keepdims=True) for at in range(0, k_dev, 128)
    ]
    noise = noise + jnp.concatenate(plain, axis=1)
    for c in range(2):
        at = c * k_dev
        right = matmul(shuffle, prj[:, at : at + k_dev], ((1,), (0,)))
        cross = jnp.sum(right[:half] * away[:half, at : at + k_dev], axis=0, keepdims=True)
        cross = cross + jnp.sum(right[half:] * mine[:half, at : at + k_dev], axis=0, keepdims=True)
        noise = noise - 2.0 * cross
    noise = noise * (1.0 / total)
    for ref in (away, mine):
        ref[half:] = jnp.zeros((8, 2 * k_dev), F32)
        ref[half : half + 1, :k_dev] = noise


def pack_kernel(mine, got, chunks):
    half = mine.shape[0] - 8
    k_dev = mine.shape[1] // 2
    data = mine[:half] + got[:half]
    tail = mine[half : half + 1, :k_dev] + got[half : half + 1, :k_dev]
    e_half = exponent(data)
    e_tail = exponent(tail)
    data = data * jnp.exp2(TOP - e_half)
    tail = tail * jnp.exp2(TOP - e_tail)
    wide = k_dev // 5
    side = [tail[:, n * wide : (n + 1) * wide] for n in range(5)]
    side = side + [jnp.broadcast_to(v, (1, wide)) for v in (e_half, e_tail, e_tail)]
    side = jnp.concatenate(side, axis=0)
    for d in range(NY):
        chunks[d, :, : 2 * k_dev] = data[8 * d : 8 * d + 8]
        low = data[8 * NY + 4 * d : 8 * NY + 4 * d + 4]
        chunks[d, :4, 2 * k_dev : 3 * k_dev] = low[:, :k_dev]
        chunks[d, 4:, 2 * k_dev : 3 * k_dev] = low[:, k_dev:]
        chunks[d, :, 3 * k_dev :] = side


def sum_kernel(owned, chunks, send, keep, last):
    k_dev = last.shape[1]
    data = jnp.zeros((8, 3 * k_dev), F32)
    tail = jnp.zeros((8, k_dev // 5), F32)
    e_half = None
    for d in range(NY):
        side = chunks[d, :, 3 * k_dev :]
        one, two = side[5:6, :1], side[6:7, :1]
        data = data + chunks[d, :, : 3 * k_dev] * jnp.exp2(one - TOP)
        tail = tail + side * jnp.exp2(two - TOP)
        e_half = one if d == 0 else jnp.maximum(e_half, one)
        e_tail = two if d == 0 else jnp.maximum(e_tail, two)
    row = jnp.concatenate([tail[n : n + 1] for n in range(5)], axis=1)
    send[:owned] = data[:owned, : 2 * k_dev] * jnp.exp2(TOP - 3.0 - e_half)
    send[owned : owned + 1, :k_dev] = row * jnp.exp2(TOP - 3.0 - e_tail)
    send[owned : owned + 1, k_dev : k_dev + 128] = jnp.broadcast_to(e_half, (1, 128))
    send[owned : owned + 1, k_dev + 128 :] = jnp.broadcast_to(e_tail, (1, k_dev - 128))
    send[owned + 1 :] = jnp.zeros((7 - owned, 2 * k_dev), F32)
    left = 8 - owned
    for c in range(2):
        at = c * k_dev
        keep[:left, at : at + k_dev] = data[owned:, at : at + k_dev]
        keep[left:owned, at : at + k_dev] = data[4 * c : 4 * c + 4, 2 * k_dev : 3 * k_dev]
    keep[owned:] = jnp.zeros((8 - owned, 2 * k_dev), F32)
    last[...] = row


def end_kernel(owned, keep, last, got, slices, spectrum):
    k_dev = last.shape[1]
    grow = jnp.exp2(got[owned : owned + 1, k_dev : k_dev + 1] - (TOP - 3.0))
    grow_tail = jnp.exp2(got[owned : owned + 1, k_dev + 128 : k_dev + 129] - (TOP - 3.0))
    out = keep[:owned] + got[:owned] * grow
    for c in range(2):
        slices[:, c, :] = out[:, c * k_dev : (c + 1) * k_dev]
    spectrum[...] = (last[...] + got[owned : owned + 1, :k_dev] * grow_tail).reshape(k_dev)


VM = pl.BlockSpec(memory_space=pltpu.VMEM)


def call(body, ins, outs, scratch=()):
    return pl.pallas_call(
        body,
        in_specs=[VM] * ins,
        out_specs=[VM] * len(outs),
        out_shape=[jax.ShapeDtypeStruct(s, t) for s, t in outs],
        scratch_shapes=list(scratch),
        compiler_params=PARAMS,
    )


def spread(v, axis, groups=None):
    return lax.all_to_all(v, axis, 0, 0, axis_index_groups=groups, tiled=True)


def img_shift(v, dh, dc):
    perm = []
    for h in range(2):
        for y in range(NY):
            for c in range(2):
                to = (h + dh) % 2 * NY + y
                perm.append(((h * NY + y) * 2 + c, to * 2 + (c + dc) % 2))
    return lax.ppermute(v, "img", perm)


def pre(images, projections, ctf_table, grp, noise_weight, sig_t):
    n_img, _, k_dev = images.shape
    orient = projections.shape[0]
    packed = (NX, sig_t.shape[0] * n_img // 128, 128)
    return call(
        pre_kernel,
        6,
        [
            (packed, F32),
            ((n_img, 2 * k_dev), BF16),
            ((n_img, k_dev), F32),
            ((orient, 3 * k_dev), BF16),
        ],
        [pltpu.VMEM((n_img, 3 * k_dev), BF16), pltpu.VMEM((n_img, k_dev), F32)],
    )(
        images.transpose(1, 0, 2),
        projections.transpose(1, 0, 2),
        ctf_table,
        grp,
        noise_weight,
        sig_t,
    )


def mid(stack, sig_t, corr, q2, prj, ctf_table, grp, total):
    orient, k_dev = prj.shape[0], ctf_table.shape[1]

    def body(*refs):
        mid_kernel(*refs[:7], total, *refs[7:])

    shape = ((orient // 2 + 8, 2 * k_dev), F32)
    return call(body, 7, [shape, shape])(stack, sig_t, corr, q2, prj, ctf_table, grp)


def per_device(images, projections, ctf_table, ctf_group, noise_weight, significant):
    img_rows, _, k_dev = images.shape
    orient = projections.shape[0]
    owned = orient // lax.axis_size("img")
    total = img_rows * lax.axis_size("img")
    sig_t = significant.T
    compact, corr, q2, prj = pre(images, projections, ctf_table, ctf_group, noise_weight, sig_t)
    along_x = [[z * NX + x for x in range(NX)] for z in range(NZ)]
    along_z = [[z * NX + x for z in range(NZ)] for x in range(NX)]
    compact = spread(compact, "blk", along_x)
    compact = call(relay_kernel, 1, [(compact.shape, F32)])(compact)[0]
    stack = spread(compact, "blk", along_z)
    away, mine = mid(stack, sig_t, corr, q2, prj, ctf_table, ctf_group, total)
    got = img_shift(away, 0, 1)
    shape = (8, 3 * k_dev + k_dev // 5)
    chunks = call(pack_kernel, 2, [((NY,) + shape, F32)])(mine, got)[0]
    along_y = [[(h * NY + y) * 2 + c for y in range(NY)] for h in range(2) for c in range(2)]
    chunks = spread(chunks.astype(F16), "img", along_y).astype(F32)
    wide = (8, 2 * k_dev)

    def add(*refs):
        sum_kernel(owned, *refs)

    def end(*refs):
        end_kernel(owned, *refs)

    send, keep, last = call(add, 1, [(wide, F32), (wide, F32), ((1, k_dev), F32)])(chunks)
    got = img_shift(send.astype(F16), 1, 0).astype(F32)
    slices, spectrum = call(end, 3, [((owned, 2, k_dev), F32), ((k_dev,), F32)])(keep, last, got)
    return (slices, spectrum)


def solution(mesh):
    return jax.shard_map(
        per_device,
        mesh=mesh,
        in_specs=(
            P("img", None, "blk"),
            P(None, None, "blk"),
            P(None, "blk"),
            P("img"),
            P("blk"),
            P("img", None),
        ),
        out_specs=(P("img", None, "blk"), P("blk")),
        check_vma=False,
    )
```

time: 82.8 us -> 73 us (0.88)
  local copies, waits for them, and re-layouts: 9.11 us -> 2.63 us
  starting transfers between devices: 5.53 us -> 10.1 us
  waiting for transfers between devices: 8.59 us -> 4.61 us
  Pallas kernels: 7.67 us -> 5.74 us
  other arithmetic: 1.59 us -> 0.14 us
    ppermute x1 -> x2, starting transfers between devices: 1.92 us -> 10.1 us  [img_shift(): return lax.ppermute(v, 'img', perm)]
    all_to_all x1 -> x0, waiting for transfers between devices: 5.94 us -> none  [spread(): return lax.all_to_all(v, axis, 0, 0, axis_index_groups=groups, tiled=True)]
    unnamed x22 -> x12, local copies, waits for them, and re-layouts: 8.42 us -> 2.63 us
    all_to_all x1 -> x0, starting transfers between devices: 3.61 us -> none  [spread(): return lax.all_to_all(v, axis, 0, 0, axis_index_groups=groups, tiled=True)]
    ppermute x1 -> x2, waiting for transfers between devices: 2.65 us -> 4.61 us  [img_shift(): return lax.ppermute(v, 'img', perm)]
    pallas_call x5 -> x6, Pallas kernels: 7.67 us -> 5.74 us  [the longest x1 2.57 us: mid(): call(body, 7, [shape, shape])(stack, sig_t, corr, q2, prj, ctf_table, grp)]
    add x1 -> x0, other arithmetic: 0.83 us -> none  [targets(): return (owner * owned + h % owned)[:, None]]
    all_to_all x2 -> x3, blocking collectives: 49.1 us -> 48.7 us  [spread(): return lax.all_to_all(v, axis, 0, 0, axis_index_groups=groups, tiled=True)]
  transfers between devices with their start and end apart: 2 -> 2, of which waited for: 2 -> 2; matrix products, arithmetic and copies ran while one was open for 1% -> 0% of each run, Pallas kernels for 0% -> 0%
where the time goes in v2:
time: 73 us; the launch traced here: 72.7 us
  blocking collectives  48.7 us (67%)
  starting transfers between devices  10.1 us (14%)
  Pallas kernels  5.74 us (8%)
  waiting for transfers between devices  4.61 us (6%)
  local copies, waits for them, and re-layouts  2.63 us (4%)
  between operations  0.74 us (1%)
    all_to_all x3, blocking collectives, spread(): return lax.all_to_all(v, axis, 0, 0, axis_index_groups=groups, tiled=True)  48.7 us
    ppermute x2, starting transfers between devices, img_shift(): return lax.ppermute(v, 'img', perm)  10.1 us
    ppermute x2, waiting for transfers between devices, img_shift(): return lax.ppermute(v, 'img', perm)  4.61 us
    unnamed x12, local copies, waits for them, and re-layouts  2.63 us
    pallas_call x1, Pallas kernels, mid(): call(body, 7, [shape, shape])(stack, sig_t, corr, q2, prj, ctf_table, grp)  2.57 us
    pallas_call x1, Pallas kernels, pre(): call(pre_kernel, 6, [(packed, F32), ((n_img, 2 * k_dev), BF16), ((n_img,...  1.94 us
  transfers between devices with their start and end apart: 2, of which 2 were waited for; matrix products, arithmetic and copies ran while one was open for 0% of the time, Pallas kernels for 0%

profile of v2, /device:TPU:2, one launch (start us, length us, event | category | flops | bytes accessed | tf_op | source)
XLA Modules:
  0.0 72.7 jit_solution(10876281532760120958)
XLA Ops:
  0.6 0.0 copy-start.4
  0.6 1.4 %copy.13 = bf16[192,2,1280]{2,0,1:T(8,128)(2,1)S(1)} copy(bf16[192,2,1280]{2,1,0:T(2,128)(2,1)} %param.7) | data formatting | bytes 1966080 | tf_op args[1]
  2.1 0.3 copy-done.4
  2.4 0.0 copy-start
  2.4 0.0 copy-start.1
  2.4 0.2 copy.12
  2.5 0.7 copy-done
  3.2 0.0 copy-done.1
  3.3 0.0 copy-done.2
  3.3 0.0 copy-done.3
  3.3 1.9 %shard_map.77 = (f32[4,120,128]{2,1,0:T(8,128)S(1)}, bf16[320,2560]{1,0:T(8,128)(2,1)S(1)}, f32[320,1280]{1,0:T(8,128)S(1)}, bf16[192,3840]{1,0:T(8,128)(2,1)S(1)}) custom-call(bf16[2,320,1280]{2,1,0:T(8,128)(2,1)S(1)} %bitcast.7, bf16[2,192,1280]{2,1,0:T(8,128)(2,1)S(1)} %bitcast.8, f32[16,1280]{1,0:T(8,128)S(1)} %copy-done, s32[320]{0:T(512)S(1)} %copy-done.3, ...), custom_call_target="tpu_custom_call" | custom-call | tf_op jit(solution)/shard_map/pallas_call | solution.py:232
  5.2 13.4 %all_to_all.15.stack = f32[4,120,128]{2,1,0:T(8,128)S(1)} all-to-all(f32[4,120,128]{2,1,0:T(8,128)S(1)} %get-tuple-element.11), channel_id=1, replica_groups={{0,1,2,3},{4,5,6,7},{8,9,10,11},{12,13,14,15},{16,17,18,19},{20,21,22,2..., dimensions={0} | all-to-all | bytes 491520 | tf_op jit(solution)/shard_map/all_to_all | solution.py:215
  18.7 10.5 %all_to_all.16.refs_0_ = f32[4,120,128]{2,1,0:T(8,128)S(1)} all-to-all(f32[4,120,128]{2,1,0:T(8,128)S(1)} %shard_map.78), channel_id=1, replica_groups={{0,4,8,12},{1,5,9,13},{2,6,10,14},{3,7,11,15},{16,20,24,28},{17,21,25,2..., dimensions={0} | all-to-all | bytes 491520 | tf_op jit(solution)/shard_map/all_to_all | solution.py:215
  29.2 2.6 %shard_map.79 = (f32[104,2560]{1,0:T(8,128)S(1)}, f32[104,2560]{1,0:T(8,128)S(1)}) custom-call(f32[4,120,128]{2,1,0:T(8,128)S(1)} %all_to_all.16.refs_0_, s32[48,320]{1,0:T(8,128)S(1)} %bitcast.10, bf16[320,2560]{1,0:T(8,128)(2,1)S(1)} %get-tuple-element.12.refs_2_, f32[320,1280]{1,0:T(8,128)S(1)} %get-tuple-element.13.refs_3_, ...), custom_call_target="tpu_custom_call" | custom-call | tf_op jit(solution)/shard_map/pallas_call | solution.py:259
  31.8 1.9 %collective-permute-start = (f32[104,2560]{1,0:T(8,128)S(1)}, f32[104,2560]{1,0:T(8,128)S(1)}, u32[]{:S(2)}, u32[]{:S(2)}) collective-permute-start(f32[104,2560]{1,0:T(8,128)S(1)} %get-tuple-element.16), channel_id=1, source_target_pairs={{0,16},{16,0},{32,48},{48,32},{64,80},{80,64},{96,112},{112,96},{1... | collective-permute-start | bytes 3194888 | tf_op jit(solution)/shard_map/ppermute | solution.py:225
  33.7 2.6 %collective-permute-done.got = f32[104,2560]{1,0:T(8,128)S(1)} collective-permute-done((f32[104,2560]{1,0:T(8,128)S(1)}, f32[104,2560]{1,0:T(8,128)S(1)}, u32[]{:S(2)}, u32[]{:S(2)}) %collective-permute-start) | collective-permute-done | bytes 1064992 | tf_op jit(solution)/shard_map/ppermute | solution.py:225
  36.4 0.3 shard_map.80
  36.7 0.1 convert_element_type.12
  36.8 24.7 %all_to_all.17 = f16[8,8,4096]{2,1,0:T(8,128)(2,1)S(1)} all-to-all(f16[8,8,4096]{2,1,0:T(8,128)(2,1)S(1)} %convert_element_type.12), channel_id=1, replica_groups={{0,32,64,96,128,160,192,224},{16,48,80,112,144,176,208,240},{256,288,32..., dimensions={0} | all-to-all | bytes 1048576 | tf_op jit(solution)/shard_map/all_to_all | solution.py:215
  61.5 0.1 convert_element_type.13.refs_0_
  61.6 0.1 shard_map.81
  61.7 8.2 %collective-permute-start.1 = (f16[8,2560]{1,0:T(8,128)(2,1)S(1)}, f16[8,2560]{1,0:T(8,128)(2,1)S(1)}, u32[]{:S(2)}, u32[]{:S(2)}) collective-permute-start(f16[8,2560]{1,0:T(8,128)(2,1)S(1)} %convert_element_type.14), channel_id=1, source_target_pairs={{0,256},{16,272},{32,288},{48,304},{64,320},{80,336},{96,352},{112... | collective-permute-start | bytes 122888 | tf_op jit(solution)/shard_map/ppermute | solution.py:225
  70.0 2.0 %collective-permute-done.1 = f16[8,2560]{1,0:T(8,128)(2,1)S(1)} collective-permute-done((f16[8,2560]{1,0:T(8,128)(2,1)S(1)}, f16[8,2560]{1,0:T(8,128)(2,1)S(1)}, u32[]{:S(2)}, u32[]{:S(2)}) %collective-permute-start.1) | collective-permute-done | bytes 40992 | tf_op jit(solution)/shard_map/ppermute | solution.py:225
  71.9 0.7 %shard_map.82 = (f32[6,2,1280]{2,1,0:T(2,128)}, f32[1280]{0:T(1024)}) custom-call(f32[8,2560]{1,0:T(8,128)S(1)} %get-tuple-element.17.refs_0_, f32[1,1280]{1,0:T(1,128)S(1)} %get-tuple-element.18.refs_1_, f32[8,2560]{1,0:T(8,128)S(1)} %convert_element_type.15.refs_2_), custom_call_target="tpu_custom_call" | custom-call | tf_op jit(solution)/shard_map/pallas_call | solution.py:290
  (5 shorter events, 0.0 us)
Async XLA Ops:
  0.6 1.7 %copy-start.4 = (bf16[320,2,1280]{2,1,0:T(2,128)(2,1)S(1)}, bf16[320,2,1280]{2,1,0:T(2,128)(2,1)}, u32[]{:S(2)}) copy-start(bf16[320,2,1280]{2,1,0:T(2,128)(2,1)} %param.6) | copy-start | bytes 4915204
  2.4 0.9 %copy-start = (f32[16,1280]{1,0:T(8,128)S(1)}, f32[16,1280]{1,0:T(8,128)}, u32[]{:S(2)}) copy-start(f32[16,1280]{1,0:T(8,128)} %refs_5_.1) | copy-start | bytes 245764
  2.4 0.9 %copy-start.1 = (s32[320,48]{0,1:T(8,128)S(1)}, s32[320,48]{0,1:T(8,128)}, u32[]{:S(2)}) copy-start(s32[320,48]{0,1:T(8,128)} %param.11) | copy-start | bytes 184324
  2.4 0.9 %copy-start.2 = (f32[1280]{0:T(1024)S(1)}, f32[1280]{0:T(1024)}, u32[]{:S(2)}) copy-start(f32[1280]{0:T(1024)} %noise.1) | copy-start | bytes 15364
  2.4 0.9 %copy-start.3 = (s32[320]{0:T(512)S(1)}, s32[320]{0:T(512)}, u32[]{:S(2)}) copy-start(s32[320]{0:T(512)} %refs_6_.1) | copy-start | bytes 3844
  31.8 4.6 %collective-permute-start = (f32[104,2560]{1,0:T(8,128)S(1)}, f32[104,2560]{1,0:T(8,128)S(1)}, u32[]{:S(2)}, u32[]{:S(2)}) collective-permute-start(f32[104,2560]{1,0:T(8,128)S(1)} %get-tuple-element.16), channel_id=1, source_target_pairs={{0,16},{16,0},{32,48},{48,32},{64,80},{80,64},{96,112},{112,96},{1... | collective-permute-start | bytes 3194888 | tf_op jit(solution)/shard_map/ppermute | solution.py:225
  61.7 10.2 %collective-permute-start.1 = (f16[8,2560]{1,0:T(8,128)(2,1)S(1)}, f16[8,2560]{1,0:T(8,128)(2,1)S(1)}, u32[]{:S(2)}, u32[]{:S(2)}) collective-permute-start(f16[8,2560]{1,0:T(8,128)(2,1)S(1)} %convert_element_type.14), channel_id=1, source_target_pairs={{0,256},{16,272},{32,288},{48,304},{64,320},{80,336},{96,352},{112... | collective-permute-start | bytes 122888 | tf_op jit(solution)/shard_map/ppermute | solution.py:225

commit v3 on v2

--- a/solution.py
+++ b/solution.py
@@ -7,6 +7,8 @@
 
 NX, NZ, NY = 4, 4, 8
 TOP = 13.0
+ORDER = (0, 4, 2, 6, 1, 5, 3, 7)
+FOUR = (0, 2, 1, 3)
 F32 = jnp.float32
 BF16 = jnp.bfloat16
 F16 = jnp.float16
@@ -87,7 +89,8 @@
     d = jnp.where(h < 8 * NY, h >> 3, (h - 8 * NY) >> 2)
     q = jnp.where(h < 8 * NY, h & 7, 8 + (h & 3))
     b = jnp.where(q < owned, 0, 1)
-    owner = (((my_h + 1 - b) & 1) * NY + d) * 2 + ((my_c + 1 - a) & 1)
+    y = ((d & 1) << 2) + (d & 2) + (d >> 2)
+    owner = (((my_h + 1 - b) & 1) * NY + y) * 2 + ((my_c + 1 - a) & 1)
     return owner * owned + q - b * owned
 
 
@@ -134,16 +137,24 @@
         cross = cross + jnp.sum(right[half:] * mine[:half, at : at + k_dev], axis=0, keepdims=True)
         noise = noise - 2.0 * cross
     noise = noise * (1.0 / total)
-    for ref in (away, mine):
-        ref[half:] = jnp.zeros((8, 2 * k_dev), F32)
-        ref[half : half + 1, :k_dev] = noise
+    e_half = exponent(away[:half])
+    e_tail = exponent(noise)
+    away[:half] = away[:half] * jnp.exp2(TOP - e_half)
+    away[half:] = jnp.zeros((8, 2 * k_dev), F32)
+    away[half : half + 1, :k_dev] = noise * jnp.exp2(TOP - e_tail)
+    away[half : half + 1, k_dev : k_dev + 128] = jnp.broadcast_to(e_half, (1, 128))
+    away[half : half + 1, k_dev + 128 :] = jnp.broadcast_to(e_tail, (1, k_dev - 128))
+    mine[half:] = jnp.zeros((8, 2 * k_dev), F32)
+    mine[half : half + 1, :k_dev] = noise
 
 
 def pack_kernel(mine, got, chunks):
     half = mine.shape[0] - 8
     k_dev = mine.shape[1] // 2
-    data = mine[:half] + got[:half]
-    tail = mine[half : half + 1, :k_dev] + got[half : half + 1, :k_dev]
+    e_half = got[half : half + 1, k_dev : k_dev + 1]
+    e_tail = got[half : half + 1, k_dev + 128 : k_dev + 129]
+    data = mine[:half] + got[:half] * jnp.exp2(e_half - TOP)
+    tail = mine[half : half + 1, :k_dev] + got[half : half + 1, :k_dev] * jnp.exp2(e_tail - TOP)
     e_half = exponent(data)
     e_tail = exponent(tail)
     data = data * jnp.exp2(TOP - e_half)
@@ -266,16 +277,16 @@
     total = img_rows * lax.axis_size("img")
     sig_t = significant.T
     compact, corr, q2, prj = pre(images, projections, ctf_table, ctf_group, noise_weight, sig_t)
-    along_x = [[z * NX + x for x in range(NX)] for z in range(NZ)]
-    along_z = [[z * NX + x for z in range(NZ)] for x in range(NX)]
+    along_x = [[z * NX + x for x in FOUR] for z in range(NZ)]
+    along_z = [[z * NX + x for z in FOUR] for x in range(NX)]
     compact = spread(compact, "blk", along_x)
     compact = call(relay_kernel, 1, [(compact.shape, F32)])(compact)[0]
     stack = spread(compact, "blk", along_z)
     away, mine = mid(stack, sig_t, corr, q2, prj, ctf_table, ctf_group, total)
-    got = img_shift(away, 0, 1)
+    got = img_shift(away.astype(F16), 0, 1).astype(F32)
     shape = (8, 3 * k_dev + k_dev // 5)
     chunks = call(pack_kernel, 2, [((NY,) + shape, F32)])(mine, got)[0]
-    along_y = [[(h * NY + y) * 2 + c for y in range(NY)] for h in range(2) for c in range(2)]
+    along_y = [[(h * NY + y) * 2 + c for y in ORDER] for h in range(2) for c in range(2)]
     chunks = spread(chunks.astype(F16), "img", along_y).astype(F32)
     wide = (8, 2 * k_dev)
 

time: 73 us -> 71.4 us (0.978)
  the two profiles are of different devices: /device:TPU:2 before, /device:TPU:16 now
where the time goes in v3:
time: 71.4 us; the launch traced here: 71.1 us
  blocking collectives  47.4 us (66%)
  starting transfers between devices  10.1 us (14%)
  Pallas kernels  5.98 us (8%)
  waiting for transfers between devices  3.85 us (5%)
  local copies, waits for them, and re-layouts  2.63 us (4%)
  between operations  0.75 us (1%)
    all_to_all x3, blocking collectives, spread(): return lax.all_to_all(v, axis, 0, 0, axis_index_groups=groups, tiled=True)  47.4 us
    ppermute x2, starting transfers between devices, img_shift(): return lax.ppermute(v, 'img', perm)  10.1 us
    ppermute x2, waiting for transfers between devices, img_shift(): return lax.ppermute(v, 'img', perm)  3.85 us
    pallas_call x1, Pallas kernels, mid(): call(body, 7, [shape, shape])(stack, sig_t, corr, q2, prj, ctf_table, grp)  2.77 us
    unnamed x12, local copies, waits for them, and re-layouts  2.63 us
    pallas_call x1, Pallas kernels, pre(): call(pre_kernel, 6, [(packed, F32), ((n_img, 2 * k_dev), BF16), ((n_img,...  1.94 us
  transfers between devices with their start and end apart: 2, of which 2 were waited for; matrix products, arithmetic and copies ran while one was open for 0% of the time, Pallas kernels for 0%

profile of v3, /device:TPU:16, one launch (start us, length us, event | category | flops | bytes accessed | tf_op | source)
XLA Modules:
  0.0 71.1 jit_solution(11593849830447787491)
XLA Ops:
  0.6 0.0 copy-start.4
  0.6 1.4 %copy.13 = bf16[192,2,1280]{2,0,1:T(8,128)(2,1)S(1)} copy(bf16[192,2,1280]{2,1,0:T(2,128)(2,1)} %param.7) | data formatting | bytes 1966080 | tf_op args[1]
  2.1 0.3 copy-done.4
  2.4 0.2 copy.12
  2.5 0.7 copy-done
  3.2 0.0 copy-done.1
  3.3 0.0 copy-done.2
  3.3 0.0 copy-done.3
  3.3 1.9 %shard_map.77 = (f32[4,120,128]{2,1,0:T(8,128)S(1)}, bf16[320,2560]{1,0:T(8,128)(2,1)S(1)}, f32[320,1280]{1,0:T(8,128)S(1)}, bf16[192,3840]{1,0:T(8,128)(2,1)S(1)}) custom-call(bf16[2,320,1280]{2,1,0:T(8,128)(2,1)S(1)} %bitcast.7, bf16[2,192,1280]{2,1,0:T(8,128)(2,1)S(1)} %bitcast.8, f32[16,1280]{1,0:T(8,128)S(1)} %copy-done, s32[320]{0:T(512)S(1)} %copy-done.3, ...), custom_call_target="tpu_custom_call" | custom-call | tf_op jit(solution)/shard_map/pallas_call | solution.py:243
  5.2 10.4 %all_to_all.15.stack = f32[4,120,128]{2,1,0:T(8,128)S(1)} all-to-all(f32[4,120,128]{2,1,0:T(8,128)S(1)} %get-tuple-element.11), channel_id=1, replica_groups={{0,2,1,3},{4,6,5,7},{8,10,9,11},{12,14,13,15},{16,18,17,19},{20,22,21,2..., dimensions={0} | all-to-all | bytes 491520 | tf_op jit(solution)/shard_map/all_to_all | solution.py:226
  15.7 14.4 %all_to_all.16.refs_0_ = f32[4,120,128]{2,1,0:T(8,128)S(1)} all-to-all(f32[4,120,128]{2,1,0:T(8,128)S(1)} %shard_map.78), channel_id=1, replica_groups={{0,8,4,12},{1,9,5,13},{2,10,6,14},{3,11,7,15},{16,24,20,28},{17,25,21,2..., dimensions={0} | all-to-all | bytes 491520 | tf_op jit(solution)/shard_map/all_to_all | solution.py:226
  30.0 2.8 %shard_map.79 = (f32[104,2560]{1,0:T(8,128)S(1)}, f32[104,2560]{1,0:T(8,128)S(1)}) custom-call(f32[4,120,128]{2,1,0:T(8,128)S(1)} %all_to_all.16.refs_0_, s32[48,320]{1,0:T(8,128)S(1)} %bitcast.10, bf16[320,2560]{1,0:T(8,128)(2,1)S(1)} %get-tuple-element.12.refs_2_, f32[320,1280]{1,0:T(8,128)S(1)} %get-tuple-element.13.refs_3_, ...), custom_call_target="tpu_custom_call" | custom-call | tf_op jit(solution)/shard_map/pallas_call | solution.py:270
  32.8 0.1 convert_element_type.18
  32.9 1.9 %collective-permute-start = (f16[104,2560]{1,0:T(8,128)(2,1)S(1)}, f16[104,2560]{1,0:T(8,128)(2,1)S(1)}, u32[]{:S(2)}, u32[]{:S(2)}) collective-permute-start(f16[104,2560]{1,0:T(8,128)(2,1)S(1)} %convert_element_type.18), channel_id=1, source_target_pairs={{0,16},{16,0},{32,48},{48,32},{64,80},{80,64},{96,112},{112,96},{1... | collective-permute-start | bytes 1597448 | tf_op jit(solution)/shard_map/ppermute | solution.py:236
  34.8 1.9 %collective-permute-done = f16[104,2560]{1,0:T(8,128)(2,1)S(1)} collective-permute-done((f16[104,2560]{1,0:T(8,128)(2,1)S(1)}, f16[104,2560]{1,0:T(8,128)(2,1)S(1)}, u32[]{:S(2)}, u32[]{:S(2)}) %collective-permute-start) | collective-permute-done | bytes 532512 | tf_op jit(solution)/shard_map/ppermute | solution.py:236
  36.7 0.1 convert_element_type.19.got
  36.8 0.4 shard_map.80
  37.2 0.1 convert_element_type.20
  37.2 22.7 %all_to_all.17 = f16[8,8,4096]{2,1,0:T(8,128)(2,1)S(1)} all-to-all(f16[8,8,4096]{2,1,0:T(8,128)(2,1)S(1)} %convert_element_type.20), channel_id=1, replica_groups={{0,128,64,192,32,160,96,224},{16,144,80,208,48,176,112,240},{256,384,32..., dimensions={0} | all-to-all | bytes 1048576 | tf_op jit(solution)/shard_map/all_to_all | solution.py:226
  59.9 0.1 convert_element_type.21.refs_0_
  60.0 0.1 shard_map.81
  60.1 8.2 %collective-permute-start.1 = (f16[8,2560]{1,0:T(8,128)(2,1)S(1)}, f16[8,2560]{1,0:T(8,128)(2,1)S(1)}, u32[]{:S(2)}, u32[]{:S(2)}) collective-permute-start(f16[8,2560]{1,0:T(8,128)(2,1)S(1)} %convert_element_type.22), channel_id=1, source_target_pairs={{0,256},{16,272},{32,288},{48,304},{64,320},{80,336},{96,352},{112... | collective-permute-start | bytes 122888 | tf_op jit(solution)/shard_map/ppermute | solution.py:236
  68.4 2.0 %collective-permute-done.1 = f16[8,2560]{1,0:T(8,128)(2,1)S(1)} collective-permute-done((f16[8,2560]{1,0:T(8,128)(2,1)S(1)}, f16[8,2560]{1,0:T(8,128)(2,1)S(1)}, u32[]{:S(2)}, u32[]{:S(2)}) %collective-permute-start.1) | collective-permute-done | bytes 40992 | tf_op jit(solution)/shard_map/ppermute | solution.py:236
  70.3 0.7 %shard_map.82 = (f32[6,2,1280]{2,1,0:T(2,128)}, f32[1280]{0:T(1024)}) custom-call(f32[8,2560]{1,0:T(8,128)S(1)} %get-tuple-element.17.refs_0_, f32[1,1280]{1,0:T(1,128)S(1)} %get-tuple-element.18.refs_1_, f32[8,2560]{1,0:T(8,128)S(1)} %convert_element_type.23.refs_2_), custom_call_target="tpu_custom_call" | custom-call | tf_op jit(solution)/shard_map/pallas_call | solution.py:301
  (7 shorter events, 0.0 us)
Async XLA Ops:
  0.6 1.7 %copy-start.4 = (bf16[320,2,1280]{2,1,0:T(2,128)(2,1)S(1)}, bf16[320,2,1280]{2,1,0:T(2,128)(2,1)}, u32[]{:S(2)}) copy-start(bf16[320,2,1280]{2,1,0:T(2,128)(2,1)} %param.6) | copy-start | bytes 4915204
  2.4 0.9 %copy-start = (f32[16,1280]{1,0:T(8,128)S(1)}, f32[16,1280]{1,0:T(8,128)}, u32[]{:S(2)}) copy-start(f32[16,1280]{1,0:T(8,128)} %refs_5_.1) | copy-start | bytes 245764
  2.4 0.9 %copy-start.1 = (s32[320,48]{0,1:T(8,128)S(1)}, s32[320,48]{0,1:T(8,128)}, u32[]{:S(2)}) copy-start(s32[320,48]{0,1:T(8,128)} %param.11) | copy-start | bytes 184324
  2.4 0.9 %copy-start.2 = (f32[1280]{0:T(1024)S(1)}, f32[1280]{0:T(1024)}, u32[]{:S(2)}) copy-start(f32[1280]{0:T(1024)} %noise.1) | copy-start | bytes 15364
  2.4 0.9 %copy-start.3 = (s32[320]{0:T(512)S(1)}, s32[320]{0:T(512)}, u32[]{:S(2)}) copy-start(s32[320]{0:T(512)} %refs_6_.1) | copy-start | bytes 3844
  32.9 3.8 %collective-permute-start = (f16[104,2560]{1,0:T(8,128)(2,1)S(1)}, f16[104,2560]{1,0:T(8,128)(2,1)S(1)}, u32[]{:S(2)}, u32[]{:S(2)}) collective-permute-start(f16[104,2560]{1,0:T(8,128)(2,1)S(1)} %convert_element_type.18), channel_id=1, source_target_pairs={{0,16},{16,0},{32,48},{48,32},{64,80},{80,64},{96,112},{112,96},{1... | collective-permute-start | bytes 1597448 | tf_op jit(solution)/shard_map/ppermute | solution.py:236
  60.1 10.2 %collective-permute-start.1 = (f16[8,2560]{1,0:T(8,128)(2,1)S(1)}, f16[8,2560]{1,0:T(8,128)(2,1)S(1)}, u32[]{:S(2)}, u32[]{:S(2)}) collective-permute-start(f16[8,2560]{1,0:T(8,128)(2,1)S(1)} %convert_element_type.22), channel_id=1, source_target_pairs={{0,256},{16,272},{32,288},{48,304},{64,320},{80,336},{96,352},{112... | collective-permute-start | bytes 122888 | tf_op jit(solution)/shard_map/ppermute | solution.py:236

commit v4 on v3

--- a/solution.py
+++ b/solution.py
@@ -7,7 +7,7 @@
 
 NX, NZ, NY = 4, 4, 8
 TOP = 13.0
-ORDER = (0, 4, 2, 6, 1, 5, 3, 7)
+ORDER = (0, 4, 1, 5, 2, 6, 3, 7)
 FOUR = (0, 2, 1, 3)
 F32 = jnp.float32
 BF16 = jnp.bfloat16
@@ -89,7 +89,7 @@
     d = jnp.where(h < 8 * NY, h >> 3, (h - 8 * NY) >> 2)
     q = jnp.where(h < 8 * NY, h & 7, 8 + (h & 3))
     b = jnp.where(q < owned, 0, 1)
-    y = ((d & 1) << 2) + (d & 2) + (d >> 2)
+    y = ((d & 1) << 2) + (d >> 1)
     owner = (((my_h + 1 - b) & 1) * NY + y) * 2 + ((my_c + 1 - a) & 1)
     return owner * owned + q - b * owned
 
@@ -106,14 +106,15 @@
     )
     expo = jnp.exp(scores - jnp.max(scores, axis=0, keepdims=True))
     w_c = (expo / jnp.sum(expo, axis=0, keepdims=True)).astype(BF16).astype(F32)
-    sig = sig_t[...]
+    sig = sig_t[...].astype(F32).astype(BF16)
+    w_b = w_c.astype(BF16)
     blocks = []
-    for base in range(0, orient, 64):
-        ids = lax.broadcasted_iota(jnp.int32, (64, n_img), 0) + base
-        acc = jnp.zeros((64, n_img), F32)
+    for base in range(0, orient, 96):
+        ids = (lax.broadcasted_iota(jnp.int32, (96, n_img), 0) + base).astype(F32).astype(BF16)
+        acc = jnp.zeros((96, n_img), BF16)
         for s in range(n_sig):
-            acc = jnp.where(sig[s : s + 1] == ids, w_c[s : s + 1], acc)
-        blocks.append(acc.astype(BF16))
+            acc = jnp.where(sig[s : s + 1] == ids, w_b[s : s + 1], acc)
+        blocks.append(acc)
     w_t = jnp.concatenate(blocks, axis=0)
     target = targets(lax.axis_index("img"), orient, orient // (4 * NY))
     shuffle = (target == lax.broadcasted_iota(jnp.int32, (orient, orient), 1)).astype(F32).astype(BF16)

time: 71.4 us -> 71.5 us (level)
  the two profiles are of different devices: /device:TPU:16 before, /device:TPU:8 now
where the time goes in v4:
time: 71.5 us; the launch traced here: 71.2 us
  blocking collectives  48.1 us (67%)
  starting transfers between devices  10.1 us (14%)
  Pallas kernels  5.4 us (8%)
  waiting for transfers between devices  3.85 us (5%)
  local copies, waits for them, and re-layouts  2.63 us (4%)
  between operations  0.75 us (1%)
    all_to_all x3, blocking collectives, spread(): return lax.all_to_all(v, axis, 0, 0, axis_index_groups=groups, tiled=True)  48.1 us
    ppermute x2, starting transfers between devices, img_shift(): return lax.ppermute(v, 'img', perm)  10.1 us
    ppermute x2, waiting for transfers between devices, img_shift(): return lax.ppermute(v, 'img', perm)  3.85 us
    unnamed x12, local copies, waits for them, and re-layouts  2.63 us
    pallas_call x1, Pallas kernels, mid(): call(body, 7, [shape, shape])(stack, sig_t, corr, q2, prj, ctf_table, grp)  2.19 us
    pallas_call x1, Pallas kernels, pre(): call(pre_kernel, 6, [(packed, F32), ((n_img, 2 * k_dev), BF16), ((n_img,...  1.94 us
  transfers between devices with their start and end apart: 2, of which 2 were waited for; matrix products, arithmetic and copies ran while one was open for 0% of the time, Pallas kernels for 0%

profile of v4, /device:TPU:8, one launch (start us, length us, event | category | flops | bytes accessed | tf_op | source)
XLA Modules:
  0.0 71.2 jit_solution(15423468386818986514)
XLA Ops:
  0.6 0.0 copy-start.4
  0.6 1.4 %copy.13 = bf16[192,2,1280]{2,0,1:T(8,128)(2,1)S(1)} copy(bf16[192,2,1280]{2,1,0:T(2,128)(2,1)} %param.7) | data formatting | bytes 1966080 | tf_op args[1]
  2.1 0.3 copy-done.4
  2.4 0.2 copy.12
  2.5 0.7 copy-done
  3.2 0.0 copy-done.1
  3.3 0.0 copy-done.2
  3.3 0.0 copy-done.3
  3.3 1.9 %shard_map.77 = (f32[4,120,128]{2,1,0:T(8,128)S(1)}, bf16[320,2560]{1,0:T(8,128)(2,1)S(1)}, f32[320,1280]{1,0:T(8,128)S(1)}, bf16[192,3840]{1,0:T(8,128)(2,1)S(1)}) custom-call(bf16[2,320,1280]{2,1,0:T(8,128)(2,1)S(1)} %bitcast.7, bf16[2,192,1280]{2,1,0:T(8,128)(2,1)S(1)} %bitcast.8, f32[16,1280]{1,0:T(8,128)S(1)} %copy-done, s32[320]{0:T(512)S(1)} %copy-done.3, ...), custom_call_target="tpu_custom_call" | custom-call | tf_op jit(solution)/shard_map/pallas_call | solution.py:244
  5.2 10.4 %all_to_all.15.stack = f32[4,120,128]{2,1,0:T(8,128)S(1)} all-to-all(f32[4,120,128]{2,1,0:T(8,128)S(1)} %get-tuple-element.11), channel_id=1, replica_groups={{0,2,1,3},{4,6,5,7},{8,10,9,11},{12,14,13,15},{16,18,17,19},{20,22,21,2..., dimensions={0} | all-to-all | bytes 491520 | tf_op jit(solution)/shard_map/all_to_all | solution.py:227
  15.7 14.4 %all_to_all.16.refs_0_ = f32[4,120,128]{2,1,0:T(8,128)S(1)} all-to-all(f32[4,120,128]{2,1,0:T(8,128)S(1)} %shard_map.78), channel_id=1, replica_groups={{0,8,4,12},{1,9,5,13},{2,10,6,14},{3,11,7,15},{16,24,20,28},{17,25,21,2..., dimensions={0} | all-to-all | bytes 491520 | tf_op jit(solution)/shard_map/all_to_all | solution.py:227
  30.0 2.2 %shard_map.79 = (f32[104,2560]{1,0:T(8,128)S(1)}, f32[104,2560]{1,0:T(8,128)S(1)}) custom-call(f32[4,120,128]{2,1,0:T(8,128)S(1)} %all_to_all.16.refs_0_, s32[48,320]{1,0:T(8,128)S(1)} %bitcast.10, bf16[320,2560]{1,0:T(8,128)(2,1)S(1)} %get-tuple-element.12.refs_2_, f32[320,1280]{1,0:T(8,128)S(1)} %get-tuple-element.13.refs_3_, ...), custom_call_target="tpu_custom_call" | custom-call | tf_op jit(solution)/shard_map/pallas_call | solution.py:271
  32.2 0.1 convert_element_type.18
  32.3 1.9 %collective-permute-start = (f16[104,2560]{1,0:T(8,128)(2,1)S(1)}, f16[104,2560]{1,0:T(8,128)(2,1)S(1)}, u32[]{:S(2)}, u32[]{:S(2)}) collective-permute-start(f16[104,2560]{1,0:T(8,128)(2,1)S(1)} %convert_element_type.18), channel_id=1, source_target_pairs={{0,16},{16,0},{32,48},{48,32},{64,80},{80,64},{96,112},{112,96},{1... | collective-permute-start | bytes 1597448 | tf_op jit(solution)/shard_map/ppermute | solution.py:237
  34.2 1.9 %collective-permute-done = f16[104,2560]{1,0:T(8,128)(2,1)S(1)} collective-permute-done((f16[104,2560]{1,0:T(8,128)(2,1)S(1)}, f16[104,2560]{1,0:T(8,128)(2,1)S(1)}, u32[]{:S(2)}, u32[]{:S(2)}) %collective-permute-start) | collective-permute-done | bytes 532512 | tf_op jit(solution)/shard_map/ppermute | solution.py:237
  36.1 0.1 convert_element_type.19.got
  36.2 0.4 shard_map.80
  36.6 0.1 convert_element_type.20
  36.7 23.3 %all_to_all.17 = f16[8,8,4096]{2,1,0:T(8,128)(2,1)S(1)} all-to-all(f16[8,8,4096]{2,1,0:T(8,128)(2,1)S(1)} %convert_element_type.20), channel_id=1, replica_groups={{0,128,32,160,64,192,96,224},{16,144,48,176,80,208,112,240},{256,384,28..., dimensions={0} | all-to-all | bytes 1048576 | tf_op jit(solution)/shard_map/all_to_all | solution.py:227
  60.0 0.1 convert_element_type.21.refs_0_
  60.1 0.1 shard_map.81
  60.2 8.2 %collective-permute-start.1 = (f16[8,2560]{1,0:T(8,128)(2,1)S(1)}, f16[8,2560]{1,0:T(8,128)(2,1)S(1)}, u32[]{:S(2)}, u32[]{:S(2)}) collective-permute-start(f16[8,2560]{1,0:T(8,128)(2,1)S(1)} %convert_element_type.22), channel_id=1, source_target_pairs={{0,256},{16,272},{32,288},{48,304},{64,320},{80,336},{96,352},{112... | collective-permute-start | bytes 122888 | tf_op jit(solution)/shard_map/ppermute | solution.py:237
  68.4 2.0 %collective-permute-done.1 = f16[8,2560]{1,0:T(8,128)(2,1)S(1)} collective-permute-done((f16[8,2560]{1,0:T(8,128)(2,1)S(1)}, f16[8,2560]{1,0:T(8,128)(2,1)S(1)}, u32[]{:S(2)}, u32[]{:S(2)}) %collective-permute-start.1) | collective-permute-done | bytes 40992 | tf_op jit(solution)/shard_map/ppermute | solution.py:237
  70.4 0.7 %shard_map.82 = (f32[6,2,1280]{2,1,0:T(2,128)}, f32[1280]{0:T(1024)}) custom-call(f32[8,2560]{1,0:T(8,128)S(1)} %get-tuple-element.17.refs_0_, f32[1,1280]{1,0:T(1,128)S(1)} %get-tuple-element.18.refs_1_, f32[8,2560]{1,0:T(8,128)S(1)} %convert_element_type.23.refs_2_), custom_call_target="tpu_custom_call" | custom-call | tf_op jit(solution)/shard_map/pallas_call | solution.py:302
  (7 shorter events, 0.0 us)
Async XLA Ops:
  0.6 1.7 %copy-start.4 = (bf16[320,2,1280]{2,1,0:T(2,128)(2,1)S(1)}, bf16[320,2,1280]{2,1,0:T(2,128)(2,1)}, u32[]{:S(2)}) copy-start(bf16[320,2,1280]{2,1,0:T(2,128)(2,1)} %param.6) | copy-start | bytes 4915204
  2.4 0.9 %copy-start = (f32[16,1280]{1,0:T(8,128)S(1)}, f32[16,1280]{1,0:T(8,128)}, u32[]{:S(2)}) copy-start(f32[16,1280]{1,0:T(8,128)} %refs_5_.1) | copy-start | bytes 245764
  2.4 0.9 %copy-start.1 = (s32[320,48]{0,1:T(8,128)S(1)}, s32[320,48]{0,1:T(8,128)}, u32[]{:S(2)}) copy-start(s32[320,48]{0,1:T(8,128)} %param.11) | copy-start | bytes 184324
  2.4 0.9 %copy-start.2 = (f32[1280]{0:T(1024)S(1)}, f32[1280]{0:T(1024)}, u32[]{:S(2)}) copy-start(f32[1280]{0:T(1024)} %noise.1) | copy-start | bytes 15364
  2.4 0.9 %copy-start.3 = (s32[320]{0:T(512)S(1)}, s32[320]{0:T(512)}, u32[]{:S(2)}) copy-start(s32[320]{0:T(512)} %refs_6_.1) | copy-start | bytes 3844
  32.3 3.8 %collective-permute-start = (f16[104,2560]{1,0:T(8,128)(2,1)S(1)}, f16[104,2560]{1,0:T(8,128)(2,1)S(1)}, u32[]{:S(2)}, u32[]{:S(2)}) collective-permute-start(f16[104,2560]{1,0:T(8,128)(2,1)S(1)} %convert_element_type.18), channel_id=1, source_target_pairs={{0,16},{16,0},{32,48},{48,32},{64,80},{80,64},{96,112},{112,96},{1... | collective-permute-start | bytes 1597448 | tf_op jit(solution)/shard_map/ppermute | solution.py:237
  60.2 10.2 %collective-permute-start.1 = (f16[8,2560]{1,0:T(8,128)(2,1)S(1)}, f16[8,2560]{1,0:T(8,128)(2,1)S(1)}, u32[]{:S(2)}, u32[]{:S(2)}) collective-permute-start(f16[8,2560]{1,0:T(8,128)(2,1)S(1)} %convert_element_type.22), channel_id=1, source_target_pairs={{0,256},{16,272},{32,288},{48,304},{64,320},{80,336},{96,352},{112... | collective-permute-start | bytes 122888 | tf_op jit(solution)/shard_map/ppermute | solution.py:237
